TPU v7x, 32 devices: a whole 2x2x4 slice. The times are simulated.
32 devices in a mesh: groups: 2 (over y), req: 4 (over x, core), tensor: 4 (over z).
Axes of the slice: x: 2, y: 2, z: 4, core: 2. Of those that a mesh axis runs over, the one named last changes fastest.
Arguments:
- hidden: bfloat16 [384, 24576], P(('groups', 'req'), 'tensor'), parts along dimension 0, may hold values from -6 to 6
- join_weight: bfloat16 [24576, 8192], P('tensor', 'req'), may hold values from -0.0390625 to 0.0390625
- norm_gain: bfloat16 [8192], P(('req', 'tensor')), may hold values from 0.099609375 to 1.8984375
- qkv_weight: bfloat16 [8192, 9216], P(('req', 'tensor')), may hold values from -0.0625 to 0.0625
- owner_draft_cache: bfloat16 [48, 512, 2, 512], P(('groups', 'req'), 'tensor'), parts along dimension 0, may hold values from -250 to 250
- node_count: int32 [48], P('groups'), parts along dimension 0, may hold values from 1 to 8, as said below
- owner: int32 [48], P('groups'), parts along dimension 0, may hold values from 0 to 3, as said below
- cache_len: int32 [48], P('groups'), parts along dimension 0, may hold values from 1 to 512, as said below
Outputs:
- draft_attention: bfloat16 [48, 8, 8192], P(('groups', 'req'), None, 'tensor'), parts along dimension 0
There are 2 independent parts, one for each index of `groups`. A program takes and returns all parts, laid end to end along the dimension named above; an argument that names none is the same for every part. Nothing has to cross between parts.
Inputs may be any that keep to these rules, and one draw needn't show every extreme that they name: Every owner holds exactly 6 requests. `node_count`: some request has all 8 nodes live. `cache_len`: some slot uses all 512 positions.
All inputs are finite; a program needn't handle non-finite values.
Results may differ from a plain program's by a relative error of at most 0.01655.
The roundings to bfloat16 on the way count: a program that leaves them out, or rounds other values in their place, can miss the bound.
Values may be sent and summed in bfloat16 or wider, within the bound.
A program may use at most 256 MiB of HBM per device.

v0:
```python
import jax
import jax.numpy as jnp
from jax import lax
from jax.sharding import PartitionSpec as P

DF = 8192
QUERY_HEADS = 64
KEY_VALUE_HEADS = 4
HEAD_SIZE = 128
TREE_SLOTS = 8
CACHE_BLOCK = 128
norm_eps = 1e-05


def slots(owner, request_per_owner):
    count_all = owner.shape[0]
    same_owner = owner[:, None] == owner[None, :]
    earlier = jnp.arange(count_all)[None, :] < jnp.arange(count_all)[:, None]
    ranking = jnp.sum((same_owner & earlier).astype(jnp.int32), axis=1)
    return owner * request_per_owner + ranking


def body(
    hidden, join_weight, norm_gain, qkv_weight, owner_draft_cache, node_count, owner, cache_len
):
    tensor_count = lax.axis_size("tensor")
    req_here = lax.axis_index("req")
    tensor_here = lax.axis_index("tensor")
    request_per_owner = owner_draft_cache.shape[0]
    count_all = owner.shape[0]
    slot_of = slots(owner, request_per_owner)
    slot_table = slot_of[None, :] == jnp.arange(count_all, dtype=jnp.int32)[:, None]
    rows_all = count_all * TREE_SLOTS
    hidden_all = lax.all_gather(hidden, "req", axis=0, tiled=True)
    partial_sum = jnp.dot(hidden_all, join_weight, preferred_element_type=jnp.float32)
    joined = lax.psum_scatter(partial_sum, "tensor", scatter_dimension=1, tiled=True).astype(
        jnp.bfloat16
    )
    features = joined.shape[1]
    joined = jnp.dot(
        slot_table.astype(jnp.bfloat16),
        joined.reshape(count_all, TREE_SLOTS * features),
        preferred_element_type=jnp.float32,
    ).reshape(rows_all, features)
    scaled = (joined * norm_gain.astype(jnp.float32)).astype(jnp.bfloat16)
    partial_qkv = jnp.dot(scaled, qkv_weight, preferred_element_type=jnp.float32)
    row_squares = jnp.sum(joined * joined, axis=1)
    own_qkv = lax.psum_scatter(partial_qkv, "req", scatter_dimension=0, tiled=True)
    total_squares = lax.dynamic_slice_in_dim(
        lax.psum(row_squares, ("req", "tensor")),
        req_here * request_per_owner * TREE_SLOTS,
        request_per_owner * TREE_SLOTS,
    )
    total_qkv = lax.psum(own_qkv, "tensor")
    query_key_value = (total_qkv * lax.rsqrt(total_squares[:, None] / DF + norm_eps)).astype(
        jnp.bfloat16
    )
    query_group_width = QUERY_HEADS // KEY_VALUE_HEADS
    query_rows = query_key_value[:, : QUERY_HEADS * HEAD_SIZE].reshape(
        request_per_owner, TREE_SLOTS, KEY_VALUE_HEADS, query_group_width, HEAD_SIZE
    )
    fresh_key = query_key_value[
        :, QUERY_HEADS * HEAD_SIZE : (QUERY_HEADS + KEY_VALUE_HEADS) * HEAD_SIZE
    ].reshape(request_per_owner, TREE_SLOTS, KEY_VALUE_HEADS, HEAD_SIZE)
    fresh_value = query_key_value[:, (QUERY_HEADS + KEY_VALUE_HEADS) * HEAD_SIZE :].reshape(
        request_per_owner, TREE_SLOTS, KEY_VALUE_HEADS, HEAD_SIZE
    )
    cached_key_rows = owner_draft_cache[:, :, 0].reshape(
        request_per_owner, CACHE_BLOCK, KEY_VALUE_HEADS, HEAD_SIZE
    )
    cached_value_rows = owner_draft_cache[:, :, 1].reshape(
        request_per_owner, CACHE_BLOCK, KEY_VALUE_HEADS, HEAD_SIZE
    )
    lengths = lax.dynamic_slice_in_dim(cache_len, req_here * request_per_owner, request_per_owner)
    live_all = jnp.sum(jnp.where(slot_table, node_count[None, :], 0), axis=1)
    live_slot = lax.dynamic_slice_in_dim(live_all, req_here * request_per_owner, request_per_owner)
    scale_factor = HEAD_SIZE ** (-0.5)
    positions = tensor_here * CACHE_BLOCK + jnp.arange(CACHE_BLOCK)
    cache_mask = (positions[None, :] < lengths[:, None])[:, None, None, None, :]
    score_cache = (
        jnp.einsum(
            "snkgd,spkd->snkgp", query_rows, cached_key_rows, preferred_element_type=jnp.float32
        )
        * scale_factor
    )
    score_cache = jnp.where(cache_mask, score_cache, -1e30)
    first_block = tensor_here == 0
    new_mask = (jnp.arange(TREE_SLOTS)[None, :] <= jnp.arange(TREE_SLOTS)[:, None]) & first_block
    new_mask = new_mask[None, :, None, None, :]
    score_new = (
        jnp.einsum("snkgd,smkd->snkgm", query_rows, fresh_key, preferred_element_type=jnp.float32)
        * scale_factor
    )
    score_new = jnp.where(new_mask, score_new, -1e30)
    local_top = jnp.maximum(jnp.max(score_cache, axis=-1), jnp.max(score_new, axis=-1))
    top_score = lax.pmax(local_top, "tensor")
    weight_cache = jnp.where(cache_mask, jnp.exp(score_cache - top_score[..., None]), 0.0)
    weight_new = jnp.where(new_mask, jnp.exp(score_new - top_score[..., None]), 0.0)
    denominator = jnp.sum(weight_cache, axis=-1) + jnp.sum(weight_new, axis=-1)
    accum = jnp.einsum(
        "snkgp,spkd->snkgd",
        weight_cache.astype(jnp.bfloat16),
        cached_value_rows,
        preferred_element_type=jnp.float32,
    )
    accum = accum + jnp.einsum(
        "snkgm,smkd->snkgd",
        weight_new.astype(jnp.bfloat16),
        fresh_value,
        preferred_element_type=jnp.float32,
    )
    head_cols = QUERY_HEADS * HEAD_SIZE // tensor_count
    accum_all, denom_all = lax.psum((accum, denominator), "tensor")
    result_all = (accum_all / denom_all[..., None]).reshape(
        request_per_owner, TREE_SLOTS, QUERY_HEADS * HEAD_SIZE
    )
    result = lax.dynamic_slice_in_dim(result_all, tensor_here * head_cols, head_cols, 2)
    alive = (jnp.arange(TREE_SLOTS)[None, :] < live_slot[:, None])[:, :, None]
    return jnp.where(alive, result, 0.0).astype(jnp.bfloat16)


def solution(mesh):
    return jax.shard_map(
        body,
        mesh=mesh,
        in_specs=(
            P(("groups", "req"), "tensor"),
            P("tensor", "req"),
            P(("req", "tensor")),
            P(("req", "tensor"), None),
            P(("groups", "req"), "tensor", None, None),
            P("groups"),
            P("groups"),
            P("groups"),
        ),
        out_specs=P(("groups", "req"), None, "tensor"),
        check_vma=False,
    )
```

profile of v0, /device:TPU:0, one launch (start us, length us, event | category | flops | bytes accessed | tf_op | source)
XLA Modules:
  0.0 341.3 jit_solution(7624498871045635591)
XLA Ops:
  6.5 0.7 all-gather.2.cloned.1.call-update
  7.3 0.0 reduce-scatter.3.cloned.1.call-start
  7.3 28.4 %all-gather.2.cloned.1.call-done = bf16[192,6144]{1,0:T(8,128)(2,1)} async-done(((bf16[48,6144]{1,0:T(8,128)(2,1)}), bf16[192,6144]{1,0:T(8,128)(2,1)}) %all-gather.2.cloned.1.call-update) | async-done | bytes 2359312 | tf_op jit(solution)/shard_map/all_gather | solution.py:34
  35.7 12.3 %fusion.29 = f32[192,2048]{1,0:T(8,128)} fusion(bf16[192,6144]{1,0:T(8,128)(2,1)} %all-gather.2.cloned.1.call-done, bf16[6144,2048]{1,0:T(8,128)(2,1)} %param.9), kind=kOutput, calls=%fused_computation.50 | convolution fusion | flops 4831838208 | bytes 29097984 | tf_op jit(solution)/shard_map/dot_general | solution.py:35
  48.0 0.0 reduce-scatter.3.cloned.1.call-update
  48.1 0.0 reduce-scatter.5.cloned.1.call-start
  48.1 0.6 copy-done.2
  48.7 0.2 convert_reduce_fusion
  48.9 34.6 %reduce-scatter.3.cloned.1.call-done = f32[192,512]{1,0:T(8,128)} async-done(((f32[192,2048]{1,0:T(8,128)}), f32[192,512]{1,0:T(8,128)}) %reduce-scatter.3.cloned.1.call-update) | async-done | bytes 393232 | tf_op jit(solution)/shard_map/reduce_scatter | solution.py:36
  83.5 1.0 convert_element_type.26
  84.5 0.1 reshape.90
  84.6 0.2 fusion.21
  84.8 0.1 reshape.91
  84.9 8.6 %fusion.19 = f32[192,9216]{1,0:T(8,128)} fusion(bf16[512,9216]{1,0:T(8,128)(2,1)} %param.11, f32[192,512]{1,0:T(8,128)S(1)} %reshape.91, f32[512]{0:T(512)S(1)} %convert_element_type.27), kind=kOutput, calls=%fused_computation.28 | convolution fusion | flops 1812135936 | bytes 16910336 | tf_op jit(solution)/shard_map/dot_general | solution.py:46
  93.5 0.0 reduce-scatter.5.cloned.1.call-update
  93.6 0.0 all-reduce.3.cloned.1.call-start
  93.6 62.7 %reduce-scatter.5.cloned.1.call-done = f32[48,9216]{1,0:T(8,128)} async-done(((f32[192,9216]{1,0:T(8,128)}), f32[48,9216]{1,0:T(8,128)}) %reduce-scatter.5.cloned.1.call-update) | async-done | bytes 1769488 | tf_op jit(solution)/shard_map/reduce_scatter | solution.py:48
  156.3 0.0 all-reduce.3.cloned.1.call-update
  156.3 0.0 all-reduce.5.cloned.1.call-start
  156.4 3.1 fusion.27
  159.5 4.7 %copy.33 = bf16[6,128,1,512]{1,3,0,2:T(8,128)(2,1)} copy(bf16[6,128,1,512]{3,2,1,0:T(2,128)(2,1)} %get-tuple-element.5) | data formatting | bytes 1572864
  164.1 2.6 copy.34
  166.7 0.1 dynamic_slice.13
  166.8 0.1 broadcast_compare_fusion
  166.9 0.1 multiply_reduce_fusion
  167.0 34.1 %psum.29 = f32[192]{0:T(256)S(1)} all-reduce(f32[192]{0:T(256)S(1)} %multiply_reduce_fusion), channel_id=1, replica_groups=mesh['groups'=2,'req'=4,'tensor'=4] {'req','tensor'}, use_global_device_ids=true, to_apply=%region_6.7 | all-reduce | flops 192 | bytes 1536 | tf_op jit(solution)/shard_map/psum | solution.py:50
  201.1 0.1 add_rsqrt_fusion
  201.2 34.3 %all-reduce.3.cloned.1.call-done = f32[48,9216]{1,0:T(8,128)} async-done(((f32[48,9216]{1,0:T(8,128)}), f32[48,9216]{1,0:T(8,128)}) %all-reduce.3.cloned.1.call-update) | async-done | bytes 1769488 | tf_op jit(solution)/shard_map/psum | solution.py:54
  235.5 1.6 multiply_convert_fusion
  237.1 0.1 slice.20
  237.2 2.0 fusion.28
  239.1 0.6 bitcast_reduce_fusion
  239.8 18.5 %pmax.7 = f32[6,8,4,16]{3,1,2,0:T(8,128)S(1)} all-reduce(f32[6,8,4,16]{3,1,2,0:T(8,128)S(1)} %max.5), channel_id=1, replica_groups=mesh['groups'=2,'req'=4,'tensor'=4] {'tensor'}, use_global_device_ids=true, to_apply=%region_9.10 | all-reduce | flops 3072 | bytes 24576 | tf_op jit(solution)/shard_map/pmax | solution.py:96
  258.3 1.7 fusion.6
  260.0 1.8 bitcast_add_fusion
  261.8 0.0 all-reduce.5.cloned.1.call-update
  261.8 0.6 copy-done.5
  262.5 0.1 select_reduce_fusion
  262.6 0.1 dynamic_slice.12
  262.6 0.1 iota_compare_fusion.4
  262.7 0.4 fusion.13
  263.1 0.9 fusion.4
  264.0 21.0 %psum.31 = f32[6,8,4,16]{3,1,2,0:T(8,128)S(1)} all-reduce(f32[6,8,4,16]{3,1,2,0:T(8,128)S(1)} %add.56), channel_id=1, replica_groups=mesh['groups'=2,'req'=4,'tensor'=4] {'tensor'}, use_global_device_ids=true, to_apply=%region_13.14 | all-reduce | flops 3072 | bytes 24576 | tf_op jit(solution)/shard_map/psum | solution.py:113
  285.0 46.5 %all-reduce.5.cloned.1.call-done = f32[6,8,4,16,128]{4,3,1,2,0:T(8,128)} async-done(((f32[6,8,4,16,128]{4,3,1,2,0:T(8,128)}), f32[6,8,4,16,128]{4,3,1,2,0:T(8,128)}) %all-reduce.5.cloned.1.call-update) | async-done | bytes 1572880 | tf_op jit(solution)/shard_map/psum | solution.py:113
  331.5 1.9 broadcast_divide_fusion
  333.4 0.2 copy.24
  333.6 0.3 reshape.95
  334.0 0.8 select_convert_fusion
  (17 shorter events, 0.1 us)
Async XLA Ops:
  6.5 29.2 %all-gather.2.cloned.1.call-start = ((), (), s32[]{:S(2)}) async-start(), calls=%async_computation.2 | async-start | bytes 2949120 | tf_op jit(solution)/shard_map/all_gather | solution.py:34
  7.3 76.3 %reduce-scatter.3.cloned.1.call-start = ((), (), s32[]{:S(2)}) async-start(), calls=%async_computation.3 | async-start | bytes 1966080 | tf_op jit(solution)/shard_map/reduce_scatter | solution.py:36
  48.0 0.7 copy-start.2
  48.0 0.7 copy-start.3
  48.1 108.2 %reduce-scatter.5.cloned.1.call-start = ((), (), s32[]{:S(2)}) async-start(), calls=%async_computation.4 | async-start | bytes 8847360 | tf_op jit(solution)/shard_map/reduce_scatter | solution.py:48
  93.6 62.8 %copy-start = (bf16[6,128,2,512]{3,2,1,0:T(2,128)(2,1)S(1)}, bf16[6,128,2,512]{3,2,1,0:T(2,128)(2,1)}, u32[]{:S(2)}) copy-start(bf16[6,128,2,512]{3,2,1,0:T(2,128)(2,1)} %param.12) | copy-start | bytes 4718596
  93.6 141.9 %all-reduce.3.cloned.1.call-start = ((), (), s32[]{:S(2)}) async-start(), calls=%async_computation.5 | async-start | bytes 3538944 | tf_op jit(solution)/shard_map/psum | solution.py:54
  156.3 175.2 %all-reduce.5.cloned.1.call-start = ((), (), s32[]{:S(2)}) async-start(), calls=%async_computation.6 | async-start | bytes 3145728 | tf_op jit(solution)/shard_map/psum | solution.py:113
  164.1 2.6 copy-start.4
  237.1 2.0 copy-start.1
  261.8 0.7 copy-start.5
Sparse Core Ops, SparseCore 0:
  8.9 26.7 all-gather.1
  48.2 35.2 reduce-scatter.2
  93.7 62.5 reduce-scatter.4
  158.7 76.7 all-reduce.2
  261.9 69.5 all-reduce.4
where the time goes:
time: 342 us; the launch traced here: 341 us
  waiting for transfers between devices  207 us (61%)
  blocking collectives  73.6 us (22%)
  matrix products  27.2 us (8%)
  between operations  13.3 us (4%)
  local copies, waits for them, and re-layouts  12.5 us (4%)
  other arithmetic  7.31 us (2%)
    reduce_scatter x1, waiting for transfers between devices, body(): lax.psum_scatter(partial_qkv, 'req', scatter_dimension=0, tiled=True)  62.7 us
    psum x1, waiting for transfers between devices, body(): accum_all, denom_all = lax.psum((accum, denominator), 'tensor')  46.5 us
    reduce_scatter x1, waiting for transfers between devices, body(): lax.psum_scatter(partial_sum, 'tensor', scatter_dimension=1, tiled=True)  34.6 us
    psum x1, waiting for transfers between devices, body(): total_qkv = lax.psum(own_qkv, 'tensor')  34.3 us
    psum x1, blocking collectives, body(): lax.psum(row_squares, ('req', 'tensor'))  34.1 us
    all_gather x1, waiting for transfers between devices, body(): hidden_all = lax.all_gather(hidden, 'req', axis=0, tiled=True)  28.4 us
    psum x1, blocking collectives, body(): accum_all, denom_all = lax.psum((accum, denominator), 'tensor')  21 us
    pmax x1, blocking collectives, body(): top_score = lax.pmax(local_top, 'tensor')  18.5 us
  transfers between devices with their start and end apart: 5, of which 5 were waited for; matrix products, arithmetic and copies ran while one was open for 4% of the time, Pallas kernels for 0%

commit v1 on v0

--- a/solution.py
+++ b/solution.py
@@ -31,7 +31,9 @@
     slot_of = slots(owner, request_per_owner)
     slot_table = slot_of[None, :] == jnp.arange(count_all, dtype=jnp.int32)[:, None]
     rows_all = count_all * TREE_SLOTS
-    hidden_all = lax.all_gather(hidden, "req", axis=0, tiled=True)
+    hidden_all = jnp.concatenate(
+        lax.all_to_all(jnp.stack([hidden] * lax.axis_size("req")), "req", 0, 0), axis=0
+    )
     partial_sum = jnp.dot(hidden_all, join_weight, preferred_element_type=jnp.float32)
     joined = lax.psum_scatter(partial_sum, "tensor", scatter_dimension=1, tiled=True).astype(
         jnp.bfloat16

time: 342 us -> 347 us (1.015)
  blocking collectives: 73.6 us -> 106 us
  waiting for transfers between devices: 207 us -> 179 us
    all_to_all x0 -> x1, blocking collectives: none -> 32.5 us  [body(): lax.all_to_all(jnp.stack([hidden] * lax.axis_size('req')), 'req', 0, 0)]
    all_gather x1 -> x0, waiting for transfers between devices: 28.4 us -> none  [body(): hidden_all = lax.all_gather(hidden, 'req', axis=0, tiled=True)]
  transfers between devices with their start and end apart: 5 -> 4, of which waited for: 5 -> 4; matrix products, arithmetic and copies ran while one was open for 4% -> 4% of each run, Pallas kernels for 0% -> 0%
where the time goes in v1:
time: 347 us; the launch traced here: 346 us
  waiting for transfers between devices  179 us (52%)
  blocking collectives  106 us (31%)
  matrix products  26.9 us (8%)
  local copies, waits for them, and re-layouts  13.8 us (4%)
  between operations  13.3 us (4%)
  other arithmetic  7.31 us (2%)
    reduce_scatter x1, waiting for transfers between devices, body(): lax.psum_scatter(partial_qkv, 'req', scatter_dimension=0, tiled=True)  62.8 us
    psum x1, waiting for transfers between devices, body(): accum_all, denom_all = lax.psum((accum, denominator), 'tensor')  46.5 us
    reduce_scatter x1, waiting for transfers between devices, body(): lax.psum_scatter(partial_sum, 'tensor', scatter_dimension=1, tiled=True)  34.9 us
    psum x1, waiting for transfers between devices, body(): total_qkv = lax.psum(own_qkv, 'tensor')  34.4 us
    psum x1, blocking collectives, body(): lax.psum(row_squares, ('req', 'tensor'))  34.1 us
    all_to_all x1, blocking collectives, body(): lax.all_to_all(jnp.stack([hidden] * lax.axis_size('req')), 'req', 0, 0)  32.5 us
    psum x1, blocking collectives, body(): accum_all, denom_all = lax.psum((accum, denominator), 'tensor')  21 us
    pmax x1, blocking collectives, body(): top_score = lax.pmax(local_top, 'tensor')  18.4 us
  transfers between devices with their start and end apart: 4, of which 4 were waited for; matrix products, arithmetic and copies ran while one was open for 4% of the time, Pallas kernels for 0%

profile of v1, /device:TPU:0, one launch (start us, length us, event | category | flops | bytes accessed | tf_op | source)
XLA Modules:
  0.0 346.2 jit_solution(4760492322875015030)
XLA Ops:
  6.5 1.3 stack.2
  7.9 32.5 %all_to_all.5 = bf16[4,48,6144]{2,1,0:T(8,128)(2,1)S(1)} all-to-all(bf16[4,48,6144]{2,1,0:T(8,128)(2,1)S(1)} %stack.2), channel_id=1, replica_groups=mesh['groups'=2,'req'=4,'tensor'=4] {'req'}, dimensions={0} | all-to-all | bytes 4718592 | tf_op jit(solution)/shard_map/all_to_all | solution.py:35
  40.4 12.0 %fusion.29 = f32[192,2048]{1,0:T(8,128)} fusion(bf16[192,6144]{1,0:T(8,128)(2,1)S(1)} %bitcast.60, bf16[6144,2048]{1,0:T(8,128)(2,1)} %param.9), kind=kOutput, calls=%fused_computation.50 | convolution fusion | flops 4831838208 | bytes 29097984 | tf_op jit(solution)/shard_map/dot_general | solution.py:37
  52.4 0.0 reduce-scatter.3.cloned.1.call-update
  52.4 0.0 reduce-scatter.5.cloned.1.call-start
  52.4 0.6 copy-done.2
  53.0 0.2 convert_reduce_fusion
  53.2 34.9 %reduce-scatter.3.cloned.1.call-done = f32[192,512]{1,0:T(8,128)} async-done(((f32[192,2048]{1,0:T(8,128)}), f32[192,512]{1,0:T(8,128)}) %reduce-scatter.3.cloned.1.call-update) | async-done | bytes 393232 | tf_op jit(solution)/shard_map/reduce_scatter | solution.py:38
  88.2 1.0 convert_element_type.26
  89.2 0.1 reshape.96
  89.3 0.2 fusion.21
  89.5 0.1 reshape.97
  89.6 8.6 %fusion.19 = f32[192,9216]{1,0:T(8,128)} fusion(bf16[512,9216]{1,0:T(8,128)(2,1)} %param.11, f32[192,512]{1,0:T(8,128)S(1)} %reshape.97, f32[512]{0:T(512)S(1)} %convert_element_type.27), kind=kOutput, calls=%fused_computation.28 | convolution fusion | flops 1812135936 | bytes 16910336 | tf_op jit(solution)/shard_map/dot_general | solution.py:48
  98.2 0.0 reduce-scatter.5.cloned.1.call-update
  98.2 0.0 copy-start
  98.2 0.0 all-reduce.3.cloned.1.call-start
  98.3 62.8 %reduce-scatter.5.cloned.1.call-done = f32[48,9216]{1,0:T(8,128)} async-done(((f32[192,9216]{1,0:T(8,128)}), f32[48,9216]{1,0:T(8,128)}) %reduce-scatter.5.cloned.1.call-update) | async-done | bytes 1769488 | tf_op jit(solution)/shard_map/reduce_scatter | solution.py:50
  161.1 0.0 all-reduce.3.cloned.1.call-update
  161.1 0.0 all-reduce.5.cloned.1.call-start
  161.2 3.1 fusion.27
  164.2 4.7 %copy.33 = bf16[6,128,1,512]{1,3,0,2:T(8,128)(2,1)} copy(bf16[6,128,1,512]{3,2,1,0:T(2,128)(2,1)} %get-tuple-element.5) | data formatting | bytes 1572864
  168.9 2.6 copy.34
  171.5 0.1 dynamic_slice.13
  171.6 0.1 broadcast_compare_fusion
  171.7 0.1 multiply_reduce_fusion
  171.8 34.1 %psum.29 = f32[192]{0:T(256)S(1)} all-reduce(f32[192]{0:T(256)S(1)} %multiply_reduce_fusion), channel_id=1, replica_groups=mesh['groups'=2,'req'=4,'tensor'=4] {'req','tensor'}, use_global_device_ids=true, to_apply=%region_6.7 | all-reduce | flops 192 | bytes 1536 | tf_op jit(solution)/shard_map/psum | solution.py:52
  205.9 0.1 add_rsqrt_fusion
  206.0 34.4 %all-reduce.3.cloned.1.call-done = f32[48,9216]{1,0:T(8,128)} async-done(((f32[48,9216]{1,0:T(8,128)}), f32[48,9216]{1,0:T(8,128)}) %all-reduce.3.cloned.1.call-update) | async-done | bytes 1769488 | tf_op jit(solution)/shard_map/psum | solution.py:56
  240.4 1.6 multiply_convert_fusion
  242.1 0.1 slice.20
  242.1 2.0 fusion.28
  244.1 0.6 bitcast_reduce_fusion
  244.8 18.4 %pmax.7 = f32[6,8,4,16]{3,1,2,0:T(8,128)S(1)} all-reduce(f32[6,8,4,16]{3,1,2,0:T(8,128)S(1)} %max.5), channel_id=1, replica_groups=mesh['groups'=2,'req'=4,'tensor'=4] {'tensor'}, use_global_device_ids=true, to_apply=%region_9.10 | all-reduce | flops 3072 | bytes 24576 | tf_op jit(solution)/shard_map/pmax | solution.py:98
  263.2 1.7 fusion.6
  264.9 1.8 bitcast_add_fusion
  266.7 0.0 all-reduce.5.cloned.1.call-update
  266.7 0.6 copy-done.5
  267.4 0.1 select_reduce_fusion
  267.5 0.1 dynamic_slice.12
  267.6 0.1 iota_compare_fusion.4
  267.6 0.4 fusion.13
  268.0 0.9 fusion.4
  269.0 21.0 %psum.31 = f32[6,8,4,16]{3,1,2,0:T(8,128)S(1)} all-reduce(f32[6,8,4,16]{3,1,2,0:T(8,128)S(1)} %add.56), channel_id=1, replica_groups=mesh['groups'=2,'req'=4,'tensor'=4] {'tensor'}, use_global_device_ids=true, to_apply=%region_13.14 | all-reduce | flops 3072 | bytes 24576 | tf_op jit(solution)/shard_map/psum | solution.py:115
  289.9 46.5 %all-reduce.5.cloned.1.call-done = f32[6,8,4,16,128]{4,3,1,2,0:T(8,128)} async-done(((f32[6,8,4,16,128]{4,3,1,2,0:T(8,128)}), f32[6,8,4,16,128]{4,3,1,2,0:T(8,128)}) %all-reduce.5.cloned.1.call-update) | async-done | bytes 1572880 | tf_op jit(solution)/shard_map/psum | solution.py:115
  336.5 1.9 broadcast_divide_fusion
  338.4 0.2 copy.24
  338.6 0.3 reshape.101
  338.9 0.8 select_convert_fusion
  (16 shorter events, 0.1 us)
Async XLA Ops:
  6.5 81.6 %reduce-scatter.3.cloned.1.call-start = ((), (), s32[]{:S(2)}) async-start(), calls=%async_computation.3 | async-start | bytes 1966080 | tf_op jit(solution)/shard_map/reduce_scatter | solution.py:38
  52.4 0.7 copy-start.2
  52.4 0.7 copy-start.3
  52.4 108.7 %reduce-scatter.5.cloned.1.call-start = ((), (), s32[]{:S(2)}) async-start(), calls=%async_computation.4 | async-start | bytes 8847360 | tf_op jit(solution)/shard_map/reduce_scatter | solution.py:50
  98.2 62.9 %copy-start = (bf16[6,128,2,512]{3,2,1,0:T(2,128)(2,1)S(1)}, bf16[6,128,2,512]{3,2,1,0:T(2,128)(2,1)}, u32[]{:S(2)}) copy-start(bf16[6,128,2,512]{3,2,1,0:T(2,128)(2,1)} %param.12) | copy-start | bytes 4718596
  98.2 142.2 %all-reduce.3.cloned.1.call-start = ((), (), s32[]{:S(2)}) async-start(), calls=%async_computation.5 | async-start | bytes 3538944 | tf_op jit(solution)/shard_map/psum | solution.py:56
  161.1 175.4 %all-reduce.5.cloned.1.call-start = ((), (), s32[]{:S(2)}) async-start(), calls=%async_computation.6 | async-start | bytes 3145728 | tf_op jit(solution)/shard_map/psum | solution.py:115
  168.9 2.6 copy-start.4
  242.1 2.0 copy-start.1
  266.7 0.7 copy-start.5
Sparse Core Ops, SparseCore 0:
  52.5 35.6 reduce-scatter.2
  98.3 62.6 reduce-scatter.4
  163.6 76.7 all-reduce.2
  266.9 69.5 all-reduce.4
